TPU v7x, 32 devices: a whole 2x2x4 slice. The times are simulated.
32 devices in a mesh: ens: 4 (over x, core), polar: 8 (over z, y).
Axes of the slice: x: 2, y: 2, z: 4, core: 2. Of those that a mesh axis runs over, the one named last changes fastest.
Arguments:
- field: bfloat16 [4, 48, 96, 720], P('ens', 'polar'), may hold values from -6 to 6
- target: bfloat16 [48, 96, 720], P('polar'), may hold values from -6 to 6
- slot_orders: int32 [360], replicated, may hold values from 0 to 359, each once
- analysis: bfloat16 [360, 48, 360], P('polar'), may hold values from -0.875 to 0.875
- synthesis: bfloat16 [360, 360, 48], P('polar'), may hold values from -0.3125 to 0.3125
- degree_filter: float32 [96, 360], replicated, may hold values from -4 to 4
Outputs:
- prediction: bfloat16 [4, 48, 96, 720], P('ens', 'polar')
- gradient: bfloat16 [4, 48, 96, 720], P('ens', 'polar')
Inputs may be any that keep to these rules, and one draw needn't show every extreme that they name: `slot_orders`: each slot number 0 to 359 appears once; a slot whose order is 360 or more is empty.
All inputs are finite; a program needn't handle non-finite values.
Results may differ from a plain program's by a relative error of at most 0.006.
Values may be sent and summed in bfloat16 or wider, within the bound.
A program may use at most 64 MiB of HBM per device.

v0:
```python
import math

import jax
import jax.numpy as jnp
from jax import lax
from jax.sharding import PartitionSpec as P

ENS = 4


smooth_sq = 0.25


def lon_tables(slot_orders, lon_count, degree_total):
    points = jnp.arange(lon_count, dtype=jnp.int32)
    phase = slot_orders[:, None] * points[None, :] % lon_count
    angle = phase.astype(jnp.float32) * (2.0 * math.pi / lon_count)
    live = (slot_orders < degree_total).astype(jnp.float32)[:, None]
    cosine = jnp.cos(angle) * live
    sine = jnp.sin(angle) * live
    paired = jnp.stack([cosine, -sine], 1)
    forward = (paired / math.sqrt(lon_count)).astype(jnp.bfloat16)
    inverse = (paired / math.sqrt(degree_total)).astype(jnp.bfloat16)
    return (forward, inverse)


def kernel_slope(diff):
    return diff / jnp.sqrt(diff * diff + smooth_sq)


def crps_slope(grouped, observed, group_count):
    rest = grouped.shape[1:]
    values = grouped.reshape((group_count, ENS) + rest).astype(jnp.float32)
    own_term = kernel_slope(values - observed.astype(jnp.float32)[:, None])

    def add_member(summed, other):
        return (summed + kernel_slope(values - other[:, None]), None)

    pair_sum, unused = lax.scan(add_member, jnp.zeros_like(values), jnp.moveaxis(values, 1, 0))
    slopes = (own_term - pair_sum / ENS).astype(jnp.bfloat16)
    return slopes.reshape(grouped.shape)


def body(field, target, slot_orders, analysis, synthesis, degree_filter):
    lat_count, chan_count, lon_count = (field.shape[1], field.shape[2], field.shape[3])
    slot_count = slot_orders.shape[0]
    ord_local, degree_total = (analysis.shape[0], analysis.shape[2])
    forward, inverse = lon_tables(slot_orders, lon_count, degree_total)
    flat = field.reshape(lat_count * chan_count, lon_count)
    spectral = jnp.dot(
        flat, forward.reshape(slot_count * 2, lon_count).T, preferred_element_type=jnp.float32
    ).astype(jnp.bfloat16)
    spectral = spectral.reshape(lat_count, chan_count, slot_count, 2).transpose(2, 3, 0, 1)
    offset = lax.axis_index("polar") * ord_local
    mine = lax.dynamic_slice_in_dim(slot_orders, offset, ord_local)
    degrees = jnp.arange(degree_total, dtype=jnp.int32)
    keeping = (degrees[None, :] >= mine[:, None]).astype(jnp.float32)
    slab_index = lax.axis_index("ens")
    slab_number = lax.axis_size("ens")
    group_count = slab_number // ENS
    filter_rows = lax.dynamic_slice_in_dim(
        degree_filter, slab_index // ENS * chan_count, chan_count, 0
    )
    scaling = keeping[:, None, :, None] * filter_rows.T[None, None]
    coeffs = jnp.einsum(
        "sptc,stl->splc",
        lax.all_to_all(spectral, "polar", split_axis=0, concat_axis=2, tiled=True),
        analysis,
        preferred_element_type=jnp.float32,
    )
    scaled = (coeffs * scaling).astype(jnp.bfloat16)
    bands = jnp.einsum(
        "splc,slt->sptc", scaled, synthesis, preferred_element_type=jnp.float32
    ).astype(jnp.bfloat16)
    result_value = lax.all_to_all(bands, "polar", split_axis=2, concat_axis=0, tiled=True)
    synth = jnp.einsum("sptc,spk->tck", result_value, inverse, preferred_element_type=jnp.float32)
    prediction = (field[0].astype(jnp.float32) + synth).astype(jnp.bfloat16)[None]
    width = chan_count // slab_number
    grouped = lax.all_to_all(prediction, "ens", split_axis=2, concat_axis=0, tiled=True)
    regrouped = target.reshape(lat_count, group_count, chan_count, lon_count)
    observed = lax.dynamic_slice_in_dim(regrouped, slab_index * width, width, 2).transpose(
        1, 0, 2, 3
    )
    slopes = crps_slope(grouped, observed, group_count)
    gradient = lax.all_to_all(slopes, "ens", split_axis=0, concat_axis=2, tiled=True)
    return (prediction, gradient)


def solution(mesh):
    in_specs = (
        P("ens", "polar", None, None),
        P("polar", None, None),
        P(),
        P("polar", None, None),
        P("polar", None, None),
        P(),
    )
    out_specs = (P("ens", "polar", None, None), P("ens", "polar", None, None))
    return jax.shard_map(body, mesh=mesh, in_specs=in_specs, out_specs=out_specs, check_vma=False)
```

profile of v0, /device:TPU:0, one launch (start us, length us, event | category | flops | bytes accessed | tf_op | source)
XLA Modules:
  0.0 167.0 jit_solution(11795042902430500069)
XLA Ops:
  0.6 0.0 copy-start
  0.6 0.8 compare_convert_fusion
  1.5 5.4 %cosine_multiply_fusion = (f32[360,1,720]{2,0,1:T(8,128)S(1)}, f32[360,1,720]{2,0,1:T(8,128)S(1)}) fusion(f32[360]{0:T(512)S(1)} %compare_convert_fusion, s32[360]{0:T(512)} %param.10), kind=kLoop, calls=%fused_computation.29 | loop fusion | flops 3110400 | bytes 2076480 | tf_op jit(solution)/shard_map/mul | solution.py:19
  6.9 0.0 copy-start.1
  6.9 1.0 copy-done.1
  7.9 0.2 multiply_convert_fusion.1
  8.1 1.8 %copy.22 = bf16[360,2,720]{2,1,0:T(2,128)(2,1)} copy(bf16[360,2,720]{2,0,1:T(8,128)(2,1)S(1)} %multiply_convert_fusion.1) | data formatting | bytes 2073600 | tf_op jit(solution)/shard_map/convert_element_type | solution.py:22
  9.9 3.5 %convert_element_type.105 = bf16[720,720]{1,0:T(8,128)(2,1)} reshape(bf16[360,2,720]{2,1,0:T(2,128)(2,1)} %copy.22) | data formatting | bytes 2073600 | tf_op jit(solution)/shard_map/convert_element_type | solution.py:22
  13.4 3.3 %fusion.16 = bf16[576,720]{1,0:T(8,128)(2,1)} fusion(bf16[720,720]{1,0:T(8,128)(2,1)} %convert_element_type.105, bf16[576,720]{1,0:T(8,128)(2,1)} %bitcast.91), kind=kOutput, calls=%fused_computation.20 | convolution fusion | flops 597611520 | bytes 2695680 | tf_op jit(solution)/shard_map/dot_general | solution.py:50
  16.7 2.2 %copy.23 = bf16[576,720]{0,1:T(8,128)(2,1)} copy(bf16[576,720]{1,0:T(8,128)(2,1)} %fusion.16) | data formatting | bytes 1658880 | tf_op jit(solution)/shard_map/convert_element_type | solution.py:52
  18.9 3.5 %reshape.251 = bf16[6,96,360,2]{1,0,3,2:T(8,128)(2,1)} reshape(bf16[576,720]{0,1:T(8,128)(2,1)} %copy.23) | data formatting | bytes 1658880 | tf_op jit(solution)/shard_map/reshape | solution.py:53
  22.4 3.5 %copy.24 = bf16[360,2,6,96]{3,1,2,0:T(2,128)(2,1)} copy(bf16[360,2,6,96]{3,2,1,0:T(8,128)(2,1)} %bitcast.85) | data formatting | bytes 1658880 | tf_op jit(solution)/shard_map/transpose | solution.py:53
  25.9 0.0 copy-start.6
  25.9 7.4 %all-to-all-start = ((bf16[360,2,6,96]{3,1,2,0:T(2,128)(2,1)}), bf16[360,2,6,96]{3,1,2,0:T(2,128)(2,1)}, u32[]{:S(2)}, u32[]{:S(2)}) async-start(bf16[360,2,6,96]{3,1,2,0:T(2,128)(2,1)} %copy.24), calls=%async_computation | async-start | bytes 2211840 | tf_op jit(solution)/shard_map/all_to_all | solution.py:67
  33.4 0.8 dynamic_slice.9
  34.1 0.1 fusion.30
  34.2 0.0 copy-done.6
  34.2 3.5 %broadcast_multiply_fusion = f32[45,360,96]{1,2,0:T(8,128)} fusion(f32[360,96]{0,1:T(8,128)S(1)} %bitcast.93, f32[45,360]{1,0:T(8,128)S(1)} %fusion.30), kind=kLoop, calls=%fused_computation.4 | loop fusion | flops 1555200 | bytes 6423840 | tf_op jit(solution)/shard_map/mul | solution.py:64
  37.7 22.7 %all-to-all-done = bf16[360,2,6,96]{3,1,2,0:T(2,128)(2,1)} async-done(((bf16[360,2,6,96]{3,1,2,0:T(2,128)(2,1)}), bf16[360,2,6,96]{3,1,2,0:T(2,128)(2,1)}, u32[]{:S(2)}, u32[]{:S(2)}) %all-to-all-start) | async-done | bytes 829472 | tf_op jit(solution)/shard_map/all_to_all | solution.py:67
  60.5 3.0 %copy.25 = bf16[45,2,8,6,96]{4,1,3,2,0:T(2,128)(2,1)} copy(bf16[45,2,8,6,96]{4,1,3,0,2:T(2,128)(2,1)} %bitcast.5) | data formatting | bytes 1658880 | tf_op jit(solution)/shard_map/all_to_all | solution.py:67
  63.5 0.0 copy-done
  63.5 9.5 %fusion.11 = bf16[45,2,48,96]{3,2,1,0:T(8,128)(2,1)} fusion(bf16[45,360,48]{1,2,0:T(8,128)(2,1)S(1)} %copy-done, f32[45,360,96]{1,2,0:T(8,128)} %broadcast_multiply_fusion, bf16[45,48,360]{2,1,0:T(8,128)(2,1)} %param.11, bf16[45,2,48,96]{3,1,2,0:T(2,128)(2,1)} %bitcast.89), kind=kOutput, calls=%fused_computation.17 | convolution fusion | flops 603832320 | bytes 10990080 | tf_op jit(solution)/shard_map/splc,slt->sptc/dot_general | solution.py:72
  73.0 2.1 %copy.27 = bf16[45,2,48,96]{3,1,0,2:T(2,128)(2,1)S(1)} copy(bf16[45,2,48,96]{3,2,1,0:T(8,128)(2,1)} %fusion.11) | data formatting | bytes 1658880 | tf_op jit(solution)/shard_map/convert_element_type | solution.py:74
  75.1 31.2 %all_to_all.63 = bf16[45,2,48,96]{3,1,0,2:T(2,128)(2,1)S(1)} all-to-all(bf16[45,2,48,96]{3,1,0,2:T(2,128)(2,1)S(1)} %copy.27), channel_id=1, replica_groups=mesh['ens'=4,'polar'=8] {'polar'}, dimensions={2} | all-to-all | bytes 1658880 | tf_op jit(solution)/shard_map/all_to_all | solution.py:75
  106.3 0.8 copy.29
  107.1 0.5 copy-done.2
  107.6 0.3 copy-done.5
  107.8 0.9 fusion.17
  108.8 0.0 copy-start.4
  108.8 0.9 copy-done.4
  109.7 1.5 copy.31
  111.2 3.5 %all-to-all-start.2 = ((bf16[1,6,96,720]{3,1,0,2:T(8,128)(2,1)}), bf16[1,6,96,720]{3,1,0,2:T(8,128)(2,1)S(1)}, u32[]{:S(2)}, u32[]{:S(2)}) async-start(bf16[1,6,96,720]{3,1,0,2:T(8,128)(2,1)} %copy.31), calls=%async_computation.2 | async-start | bytes 2359296 | tf_op jit(solution)/shard_map/all_to_all | solution.py:79
  114.8 1.7 %dynamic-slice_convert_fusion = f32[6,24,720]{2,1,0:T(8,128)} fusion(bf16[6,96,720]{2,1,0:T(8,128)(2,1)} %param.9, s32[]{:T(128)S(6)} %select_n.29), kind=kLoop, calls=%fused_computation.35 | loop fusion | flops 103680 | bytes 622084 | tf_op jit(solution)/shard_map/convert_element_type | solution.py:34
  116.5 14.1 %all-to-all-done.2 = bf16[1,6,96,720]{3,1,0,2:T(8,128)(2,1)S(1)} async-done(((bf16[1,6,96,720]{3,1,0,2:T(8,128)(2,1)}), bf16[1,6,96,720]{3,1,0,2:T(8,128)(2,1)S(1)}, u32[]{:S(2)}, u32[]{:S(2)}) %all-to-all-start.2) | async-done | bytes 829472 | tf_op jit(solution)/shard_map/all_to_all | solution.py:79
  130.6 1.0 copy-done.3
  131.6 1.4 copy.46
  133.1 15.8 %while.11 = (s32[]{:T(128)}, f32[1,4,6,24,720]{4,3,2,1,0:T(8,128)}, f32[4,1,6,24,720]{4,3,2,1,0:T(8,128)S(1)}, f32[1,4,6,24,720]{4,3,2,1,0:T(8,128)S(1)}, s32[]{:T(128)}, /*index=5*/s32[]{:T(128)}) while((s32[]{:T(128)}, f32[1,4,6,24,720]{4,3,2,1,0:T(8,128)}, f32[4,1,6,24,720]{4,3,2,1,0:T(8,128)S(1)}, ...), condition=%wide.region_1.2_spmd.clone, body=%wide.region_0.1_spmd.clone.sunk | while | flops 2488323 | bytes 6220883 | solution.py:39
  133.1 0.8 dynamic-slice_bitcast_fusion.2
  133.9 2.7 %select_add_fusion.2 = f32[1,4,6,24,720]{4,3,2,1,0:T(8,128)} fusion(f32[1,4,6,24,720]{4,3,2,1,0:T(8,128)} %get-tuple-element.96, f32[1,4,6,24,720]{4,3,2,1,0:T(8,128)S(1)} %get-tuple-element.104, f32[6,24,720]{2,1,0:T(8,128)} %dynamic-slice_bitcast_fusion.2, pred[]{:T(512)S(6)} %compare.5), kind=kLoop, calls=%fused_computation.clone.1 | loop fusion | flops 2488320 | bytes 5391361 | tf_op jit(solution)/shard_map/while/body/eval_jaxpr/add | solution.py:37
  136.6 0.8 dynamic-slice_bitcast_fusion.2
  137.5 3.2 %select_add_fusion.2 = f32[1,4,6,24,720]{4,3,2,1,0:T(8,128)} fusion(f32[1,4,6,24,720]{4,3,2,1,0:T(8,128)} %get-tuple-element.96, f32[1,4,6,24,720]{4,3,2,1,0:T(8,128)S(1)} %get-tuple-element.104, f32[6,24,720]{2,1,0:T(8,128)} %dynamic-slice_bitcast_fusion.2, pred[]{:T(512)S(6)} %compare.5), kind=kLoop, calls=%fused_computation.clone.1 | loop fusion | flops 2488320 | bytes 5391361 | tf_op jit(solution)/shard_map/while/body/eval_jaxpr/add | solution.py:37
  140.7 0.8 dynamic-slice_bitcast_fusion.2
  141.5 3.2 %select_add_fusion.2 = f32[1,4,6,24,720]{4,3,2,1,0:T(8,128)} fusion(f32[1,4,6,24,720]{4,3,2,1,0:T(8,128)} %get-tuple-element.96, f32[1,4,6,24,720]{4,3,2,1,0:T(8,128)S(1)} %get-tuple-element.104, f32[6,24,720]{2,1,0:T(8,128)} %dynamic-slice_bitcast_fusion.2, pred[]{:T(512)S(6)} %compare.5), kind=kLoop, calls=%fused_computation.clone.1 | loop fusion | flops 2488320 | bytes 5391361 | tf_op jit(solution)/shard_map/while/body/eval_jaxpr/add | solution.py:37
  144.8 0.8 dynamic-slice_bitcast_fusion.2
  145.6 3.2 %select_add_fusion.2 = f32[1,4,6,24,720]{4,3,2,1,0:T(8,128)} fusion(f32[1,4,6,24,720]{4,3,2,1,0:T(8,128)} %get-tuple-element.96, f32[1,4,6,24,720]{4,3,2,1,0:T(8,128)S(1)} %get-tuple-element.104, f32[6,24,720]{2,1,0:T(8,128)} %dynamic-slice_bitcast_fusion.2, pred[]{:T(512)S(6)} %compare.5), kind=kLoop, calls=%fused_computation.clone.1 | loop fusion | flops 2488320 | bytes 5391361 | tf_op jit(solution)/shard_map/while/body/eval_jaxpr/add | solution.py:37
  148.9 2.0 %fusion.29 = bf16[4,6,24,720]{3,2,1,0:T(8,128)(2,1)S(1)} fusion(f32[1,4,6,24,720]{4,3,2,1,0:T(8,128)} %get-tuple-element.24, f32[1,4,6,24,720]{4,3,2,1,0:T(8,128)S(1)} %get-tuple-element.107, f32[6,24,720]{2,1,0:T(8,128)} %dynamic-slice_convert_fusion), kind=kLoop, calls=%fused_computation.34 | loop fusion | flops 2903040 | bytes 4561920 | tf_op jit(solution)/shard_map/reshape | solution.py:41
  150.9 15.1 %all_to_all.64 = bf16[4,6,24,720]{3,2,1,0:T(8,128)(2,1)S(1)} all-to-all(bf16[4,6,24,720]{3,2,1,0:T(8,128)(2,1)S(1)} %fusion.29), channel_id=1, replica_groups=mesh['ens'=4,'polar'=8] {'ens'}, dimensions={0} | all-to-all | bytes 1658880 | tf_op jit(solution)/shard_map/all_to_all | solution.py:85
  166.0 1.0 copy.34
  (4 shorter events, 0.0 us)
Async XLA Ops:
  0.6 62.8 %copy-start = (bf16[45,360,48]{1,2,0:T(8,128)(2,1)S(1)}, bf16[45,360,48]{1,2,0:T(8,128)(2,1)}, u32[]{:S(2)}) copy-start(bf16[45,360,48]{1,2,0:T(8,128)(2,1)} %param.12) | copy-start | bytes 4665604
  6.9 1.0 copy-start.1
  25.9 8.2 %copy-start.6 = (f32[96,360]{1,0:T(8,128)S(1)}, f32[96,360]{1,0:T(8,128)}, u32[]{:S(2)}) copy-start(f32[96,360]{1,0:T(8,128)} %param.13) | copy-start | bytes 414724
  25.9 34.5 %all-to-all-start = ((bf16[360,2,6,96]{3,1,2,0:T(2,128)(2,1)}), bf16[360,2,6,96]{3,1,2,0:T(2,128)(2,1)}, u32[]{:S(2)}, u32[]{:S(2)}) async-start(bf16[360,2,6,96]{3,1,2,0:T(2,128)(2,1)} %copy.24), calls=%async_computation | async-start | bytes 2211840 | tf_op jit(solution)/shard_map/all_to_all | solution.py:67
  106.3 1.2 copy-start.2
  106.3 1.5 copy-start.5
  108.8 0.9 copy-start.4
  111.2 19.4 %all-to-all-start.2 = ((bf16[1,6,96,720]{3,1,0,2:T(8,128)(2,1)}), bf16[1,6,96,720]{3,1,0,2:T(8,128)(2,1)S(1)}, u32[]{:S(2)}, u32[]{:S(2)}) async-start(bf16[1,6,96,720]{3,1,0,2:T(8,128)(2,1)} %copy.31), calls=%async_computation.2 | async-start | bytes 2359296 | tf_op jit(solution)/shard_map/all_to_all | solution.py:79
  130.6 1.0 copy-start.3
where the time goes:
time: 168 us; the launch traced here: 167 us
  blocking collectives  46.3 us (28%)
  waiting for transfers between devices  36.8 us (22%)
  local copies, waits for them, and re-layouts  32.1 us (19%)
  other arithmetic  26.3 us (16%)
  matrix products  13.7 us (8%)
  starting transfers between devices  10.9 us (6%)
    all_to_all x1, blocking collectives, body(): lax.all_to_all(bands, 'polar', split_axis=2, concat_axis=0, tiled=True)  31.2 us
    all_to_all x1, waiting for transfers between devices, body(): lax.all_to_all(spectral, 'polar', split_axis=0, concat_axis=2, tiled=True)  22.7 us
    all_to_all x1, blocking collectives, body(): lax.all_to_all(slopes, 'ens', split_axis=0, concat_axis=2, tiled=True)  15.1 us
    all_to_all x1, waiting for transfers between devices, body(): lax.all_to_all(prediction, 'ens', split_axis=2, concat_axis=0, tiled=True)  14.1 us
    add x4, other arithmetic, add_member(): return (summed + kernel_slope(values - other[:, None]), None)  12.4 us
    dot_general x1, matrix products, body(): jnp.einsum('splc,slt->sptc', scaled, synthesis, preferred_element_type=jn...  9.52 us
    all_to_all x1, starting transfers between devices, body(): lax.all_to_all(spectral, 'polar', split_axis=0, concat_axis=2, tiled=True)  7.41 us
    mul x1, other arithmetic, lon_tables(): cosine = jnp.cos(angle) * live  5.44 us
  transfers between devices with their start and end apart: 2, of which 2 were waited for; matrix products, arithmetic and copies ran while one was open for 4% of the time, Pallas kernels for 0%

commit v1 on v0

v1 whole, which is shorter than its diff:
```python
import functools
import math

import jax
import jax.numpy as jnp
import numpy as np
from jax import lax
from jax.experimental import pallas as pl
from jax.experimental.pallas import tpu as pltpu
from jax.sharding import PartitionSpec as P

ENS = 4
SMOOTH_SQ = 0.25
MESH = pl.DeviceIdType.MESH
F32 = jnp.float32
BF16 = jnp.bfloat16
LANES = 128


def order_tables(lon_count, degree_total):
    phase = np.arange(degree_total)[:, None] * np.arange(lon_count)[None, :] % lon_count
    angle = phase.astype(np.float32) * np.float32(2.0 * math.pi / lon_count)
    paired = np.stack([np.cos(angle), -np.sin(angle)])
    forward = jnp.asarray((paired / np.float32(math.sqrt(lon_count))).astype(BF16))
    inverse = jnp.asarray((paired / np.float32(math.sqrt(degree_total))).astype(BF16))
    return forward, inverse


def nt_dot(a, b):
    return lax.dot_general(a, b, (((1,), (1,)), ((), ())), preferred_element_type=F32)


def kernel_slope(diff):
    return diff * lax.rsqrt(diff * diff + SMOOTH_SQ)


def kernel(
    sizes,
    field_ref, orders_ref, padded_ref, filter_ref, forward_ref,
    inverse_hbm, target_hbm, analysis_hbm, synthesis_hbm,
    pred_ref, grad_ref,
    inverse_tab, target_ref, analysis_ref, synthesis_ref,
    analysis_t, synthesis_t, filter_t, inverse_rows,
    send1, recv1, x0, x1, b0, b1, send2, recv2, members, slopes, grad_in,
    local_sem, send1_sem, recv1_sem, send2_sem, recv2_sem, send3_sem, recv3_sem, send4_sem, recv4_sem,
):
    n, lat, chan, lon, slots, padded, degrees, per_send, pair = sizes
    lat_total = n * lat
    me = lax.axis_index("polar")
    slab = lax.axis_index("ens")
    member = lax.rem(slab, ENS)
    group_base = slab - member
    chunks = lat // pair
    rows = pair * chan
    quarter = rows // ENS

    local = [
        pltpu.make_async_copy(src, dst, local_sem.at[i])
        for i, (src, dst) in enumerate(
            [
                (analysis_hbm, analysis_ref),
                (synthesis_hbm, synthesis_ref),
                (inverse_hbm, inverse_tab),
                (target_hbm, target_ref),
            ]
        )
    ]
    for copy in local:
        copy.start()

    barrier = pltpu.get_barrier_semaphore()

    @pl.loop(1, n)
    def _(step):
        pl.semaphore_signal(
            barrier, inc=1, device_id={"polar": lax.rem(me + step, n)}, device_id_type=MESH
        )

    for step in range(1, ENS):
        other = group_base + lax.rem(member + step, ENS)
        pl.semaphore_signal(barrier, inc=1, device_id={"ens": other}, device_id_type=MESH)
    pl.semaphore_wait(barrier, n - 1 + ENS - 1)

    def first_copy(slot, dest):
        return pltpu.make_async_remote_copy(
            src_ref=send1.at[dest],
            dst_ref=recv1.at[slot],
            send_sem=send1_sem.at[dest],
            recv_sem=recv1_sem.at[slot],
            device_id={"polar": dest},
            device_id_type=MESH,
        )

    def second_copy(slot, dest, chunk):
        return pltpu.make_async_remote_copy(
            src_ref=send2.at[chunk, dest],
            dst_ref=recv2.at[chunk, slot],
            send_sem=send2_sem.at[chunk, dest],
            recv_sem=recv2_sem.at[chunk, slot],
            device_id={"polar": dest},
            device_id_type=MESH,
        )

    def row_start(chunk, owner):
        return pl.multiple_of(chunk * rows + owner * quarter, 16)

    def member_copy(slot, dest, chunk):
        return pltpu.make_async_remote_copy(
            src_ref=pred_buf_at(chunk, dest),
            dst_ref=members.at[chunk, slot],
            send_sem=send3_sem.at[chunk, dest],
            recv_sem=recv3_sem.at[chunk, slot],
            device_id={"ens": group_base + dest},
            device_id_type=MESH,
        )

    def pred_buf_at(chunk, dest):
        return pred_ref.at[pl.ds(row_start(chunk, dest), quarter)]

    def slope_copy(slot, dest, chunk):
        return pltpu.make_async_remote_copy(
            src_ref=slopes.at[chunk, dest],
            dst_ref=grad_in.at[pl.ds(row_start(chunk, slot), quarter)],
            send_sem=send4_sem.at[chunk, dest],
            recv_sem=recv4_sem.at[chunk, slot],
            device_id={"ens": group_base + dest},
            device_id_type=MESH,
        )

    def one_hot(block):
        ids = lax.broadcasted_iota(jnp.int32, (block.shape[0], degrees), 1)
        return jnp.where(ids == block, 1.0, 0.0).astype(BF16)

    def selected(hot, table):
        return jnp.dot(hot, table, preferred_element_type=F32).astype(BF16)

    batches = n // per_send
    mine = me // per_send

    @pl.loop(0, batches)
    def _(i):
        batch = lax.rem(mine + i, batches)
        first = batch * per_send
        span = per_send * padded
        hot = one_hot(padded_ref[pl.ds(pl.multiple_of(first * padded, 16), span), :])
        real = nt_dot(selected(hot, forward_ref[0]), field_ref[...])
        imag = nt_dot(selected(hot, forward_ref[1]), field_ref[...])
        both = jnp.concatenate([real, imag], axis=1).astype(BF16)
        for j in range(per_send):
            send1[first + j] = both[j * padded : (j + 1) * padded]

        @pl.loop(0, per_send)
        def _(j):
            dest = first + lax.rem(me + j, per_send)

            @pl.when(dest != me)
            def _():
                first_copy(me, dest).start()

    local[0].wait()
    local[1].wait()
    local[2].wait()
    local[3].wait()

    @pl.loop(0, slots)
    def _(s):
        order = orders_ref[me * slots + s]
        table = jnp.transpose(analysis_ref[s].astype(F32))
        degree = lax.broadcasted_iota(jnp.int32, table.shape, 0)
        analysis_t[s] = jnp.where(degree >= order, table, 0.0).astype(BF16)
        synthesis_t[s] = jnp.transpose(synthesis_ref[s].astype(F32)).astype(BF16)

    turned = jnp.transpose(filter_ref[...])
    filter_t[...] = jnp.zeros_like(filter_t)
    filter_t[:, 0:chan] = turned
    filter_t[:, LANES : LANES + chan] = turned

    @pl.loop(0, batches)
    def _(i):
        span = per_send * padded
        at = pl.ds(pl.multiple_of(i * span, 16), span)
        hot = one_hot(padded_ref[at, :])
        inverse_rows[0, at] = selected(hot, inverse_tab[0])
        inverse_rows[1, at] = selected(hot, inverse_tab[1])

    b0[...] = jnp.zeros_like(b0)
    b1[...] = jnp.zeros_like(b1)

    recv1[me] = send1[me]

    @pl.loop(0, n)
    def _(src):
        @pl.when(src != me)
        def _():
            first_copy(src, src).wait_recv()

        block = recv1[src].astype(F32)
        for t in range(lat):
            at = pl.ds(pl.multiple_of((src * lat + t) * padded, 16), padded)
            x0[at, 0:chan] = block[:, t * chan : (t + 1) * chan]
            x1[at, 0:chan] = block[:, (lat + t) * chan : (lat + t + 1) * chan]

    def legendre(s, carry):
        at = pl.ds(s, lat_total, stride=padded)
        values = jnp.concatenate([x0[at, :], x1[at, :]], axis=1).astype(BF16)
        coeffs = jnp.dot(analysis_t[s], values, preferred_element_type=F32)
        scaled = (coeffs * filter_t[...]).astype(BF16)
        bands = jnp.dot(synthesis_t[s], scaled, preferred_element_type=F32)
        b0[at, :] = bands[:, :LANES]
        b1[at, :] = bands[:, LANES:]
        return carry

    lax.fori_loop(0, slots, legendre, 0, unroll=3 if slots % 3 == 0 else 1)

    for chunk in range(chunks):

        @pl.loop(0, n)
        def _(step):
            dest = lax.rem(me + 1 + step, n)
            parts = []
            for source in (b0, b1):
                for t in range(pair):
                    at = (dest * lat + chunk * pair + t) * padded
                    parts.append(source[pl.ds(pl.multiple_of(at, 16), padded), 0:chan])
            send2[chunk, dest] = jnp.concatenate(parts, axis=1).astype(BF16)

            @pl.when(dest != me)
            def _():
                second_copy(me, dest, chunk).start()

    def invert(chunk):
        recv2[chunk, me] = send2[chunk, me]

        @pl.loop(1, n)
        def _(step):
            src = lax.rem(me + step, n)
            second_copy(src, src, chunk).wait_recv()

        bands = recv2[chunk].reshape(n * padded, 2 * rows)
        turned = jnp.transpose(bands.astype(F32)).astype(BF16)
        synth = jnp.dot(turned[:rows], inverse_rows[0], preferred_element_type=F32)
        synth = synth + jnp.dot(turned[rows:], inverse_rows[1], preferred_element_type=F32)
        at = pl.ds(chunk * rows, rows)
        pred_ref[at, :] = (field_ref[at, :].astype(F32) + synth).astype(BF16)
        for step in range(1, ENS):
            member_copy(member, lax.rem(member + step, ENS), chunk).start()

    def score(chunk):
        own = pl.ds(row_start(chunk, member), quarter)
        members[chunk, member] = pred_ref[own, :]
        for step in range(1, ENS):
            source = lax.rem(member + step, ENS)
            member_copy(source, source, chunk).wait_recv()

        @pl.loop(0, quarter // 16)
        def _(i):
            start = pl.multiple_of(i * 16, 16)
            at = pl.ds(start, 16)
            seen = target_ref[pl.ds(row_start(chunk, member) + start, 16), :].astype(F32)
            values = [members[chunk, e, at, :].astype(F32) for e in range(ENS)]
            pairs = [jnp.zeros_like(seen) for _ in range(ENS)]
            for a in range(ENS):
                for b in range(a + 1, ENS):
                    slope = kernel_slope(values[a] - values[b])
                    pairs[a] = pairs[a] + slope
                    pairs[b] = pairs[b] - slope
            for e in range(ENS):
                total = kernel_slope(values[e] - seen) - pairs[e] / ENS
                slopes[chunk, e, at, :] = total.astype(BF16)

        for step in range(1, ENS):
            slope_copy(member, lax.rem(member + step, ENS), chunk).start()
        grad_in[own, :] = slopes[chunk, member]

    for chunk in range(chunks):
        invert(chunk)
        if chunk:
            score(chunk - 1)
    score(chunks - 1)

    for chunk in range(chunks):
        for step in range(1, ENS):
            other = lax.rem(member + step, ENS)
            slope_copy(other, other, chunk).wait_recv()
    grad_ref[...] = grad_in[...]

    @pl.loop(1, n)
    def _(step):
        dest = lax.rem(me + step, n)
        first_copy(me, dest).wait_send()
        for chunk in range(chunks):
            second_copy(me, dest, chunk).wait_send()

    for chunk in range(chunks):
        for step in range(1, ENS):
            other = lax.rem(member + step, ENS)
            member_copy(member, other, chunk).wait_send()
            slope_copy(member, other, chunk).wait_send()


def body(field, target, slot_orders, analysis, synthesis, degree_filter):
    lat, chan, lon = field.shape[1:]
    slots, lat_total, degrees = analysis.shape
    n = lax.axis_size("polar")
    group_count = lax.axis_size("ens") // ENS
    padded = -(-slots // 16) * 16
    per_send = max(d for d in range(1, n + 1) if n % d == 0 and (d == 1 or d * padded <= 192))
    pair = 2 if lat % 2 == 0 else 1
    chunks = lat // pair
    rows = pair * chan
    quarter = rows // ENS
    forward, inverse = order_tables(lon, degrees)
    padded_orders = jnp.pad(
        slot_orders.reshape(n, slots), ((0, 0), (0, padded - slots)), constant_values=-1
    ).reshape(n * padded, 1)
    observed = target
    filters = degree_filter
    if group_count > 1:
        start = lax.axis_index("ens") // ENS * chan
        observed = lax.dynamic_slice_in_dim(target, start, chan, 1)
        filters = lax.dynamic_slice_in_dim(degree_filter, start, chan, 0)
    sizes = (n, lat, chan, lon, slots, padded, degrees, per_send, pair)
    vmem = pl.BlockSpec(memory_space=pltpu.VMEM)
    smem = pl.BlockSpec(memory_space=pltpu.SMEM)
    anywhere = pl.BlockSpec(memory_space=pl.ANY)
    dma = pltpu.SemaphoreType.DMA
    flat = jax.ShapeDtypeStruct((lat * chan, lon), BF16)
    prediction, gradient = pl.pallas_call(
        functools.partial(kernel, sizes),
        out_shape=(flat, flat),
        in_specs=[vmem, smem, vmem, vmem, vmem, anywhere, anywhere, anywhere, anywhere],
        out_specs=(vmem, vmem),
        scratch_shapes=[
            pltpu.VMEM(inverse.shape, BF16),
            pltpu.VMEM((lat * chan, lon), BF16),
            pltpu.VMEM(analysis.shape, BF16),
            pltpu.VMEM(synthesis.shape, BF16),
            pltpu.VMEM((slots, degrees, lat_total), BF16),
            pltpu.VMEM((slots, lat_total, degrees), BF16),
            pltpu.VMEM((degrees, 2 * LANES), F32),
            pltpu.VMEM((2, n * padded, lon), BF16),
            pltpu.VMEM((n, padded, 2 * lat * chan), BF16),
            pltpu.VMEM((n, padded, 2 * lat * chan), BF16),
            pltpu.VMEM((lat_total * padded, LANES), F32),
            pltpu.VMEM((lat_total * padded, LANES), F32),
            pltpu.VMEM((lat_total * padded, LANES), F32),
            pltpu.VMEM((lat_total * padded, LANES), F32),
            pltpu.VMEM((chunks, n, padded, 2 * rows), BF16),
            pltpu.VMEM((chunks, n, padded, 2 * rows), BF16),
            pltpu.VMEM((chunks, ENS, quarter, lon), BF16),
            pltpu.VMEM((chunks, ENS, quarter, lon), BF16),
            pltpu.VMEM((lat * chan, lon), BF16),
            dma((4,)),
            dma((n,)),
            dma((n,)),
            dma((chunks, n)),
            dma((chunks, n)),
            dma((chunks, ENS)),
            dma((chunks, ENS)),
            dma((chunks, ENS)),
            dma((chunks, ENS)),
        ],
        compiler_params=pltpu.CompilerParams(
            collective_id=0, has_side_effects=True, vmem_limit_bytes=56 * 1024 * 1024
        ),
    )(
        field.reshape(lat * chan, lon),
        slot_orders,
        padded_orders,
        filters,
        forward,
        inverse,
        observed.reshape(lat * chan, lon),
        analysis,
        synthesis,
    )
    return prediction.reshape(field.shape), gradient.reshape(field.shape)


def solution(mesh):
    in_specs = (
        P("ens", "polar", None, None),
        P("polar", None, None),
        P(),
        P("polar", None, None),
        P("polar", None, None),
        P(),
    )
    out_specs = (P("ens", "polar", None, None), P("ens", "polar", None, None))
    return jax.shard_map(body, mesh=mesh, in_specs=in_specs, out_specs=out_specs, check_vma=False)
```

time: 168 us -> 88.5 us (0.53)
  the two profiles are of different devices: /device:TPU:0 before, /device:TPU:13 now
where the time goes in v1:
time: 88.5 us; the launch traced here: 88.2 us
  Pallas kernels  78.2 us (88%)
  local copies, waits for them, and re-layouts  9.36 us (11%)
    pallas_call x1, Pallas kernels, body(): pl.pallas_call(functools.partial(kernel, sizes), out_shape=(flat, flat),...  78.2 us
    unnamed x5, local copies, waits for them, and re-layouts  7.79 us

profile of v1, /device:TPU:13, one launch (start us, length us, event | category | flops | bytes accessed | tf_op | source)
XLA Modules:
  0.0 88.2 jit_solution(14835673499390727400)
XLA Ops:
  0.6 0.8 reshape.23
  1.4 0.8 reshape.28.padded_ref
  2.2 4.7 %copy.12.synthesis_hbm = bf16[45,360,48]{2,1,0:T(8,128)(2,1)} copy(bf16[45,360,48]{1,2,0:T(8,128)(2,1)} %param.12) | data formatting | bytes 3110400 | tf_op args[4]
  6.9 78.2 %shard_map.95 = (bf16[576,720]{1,0:T(8,128)(2,1)}, bf16[576,720]{1,0:T(8,128)(2,1)}) custom-call(bf16[576,720]{1,0:T(8,128)(2,1)} %bitcast.4, s32[360]{0:T(512)} %orders_ref.1, s32[384,1]{1,0:T(8,128)} %reshape.28.padded_ref, f32[96,360]{1,0:T(8,128)} %filter_ref.1, bf16[2,360,720]{2,1,0:T(8,128)(2,1)} %constant.6.clone.forward_ref, ...), custom_call_target="tpu_custom_call" | custom-call | tf_op jit(solution)/shard_map/pallas_call | solution.py:328
  85.1 0.0 copy-start
  85.1 2.2 %copy.15 = bf16[1,6,96,720]{3,2,1,0:T(8,128)(2,1)} copy(bf16[1,6,96,720]{3,2,1,0:T(8,128)(2,1)} %bitcast.7) | data formatting | bytes 1658880
  87.3 0.0 copy-done
  87.3 0.9 %copy.16 = bf16[1,6,96,720]{3,2,1,0:T(8,128)(2,1)} copy(bf16[1,6,96,720]{3,2,1,0:T(8,128)(2,1)S(1)} %bitcast.6) | data formatting | bytes 1658880
  (1 shorter events, 0.0 us)
Async XLA Ops:
  85.1 2.2 %copy-start = (bf16[576,720]{1,0:T(8,128)(2,1)S(1)}, bf16[576,720]{1,0:T(8,128)(2,1)}, u32[]{:S(2)}) copy-start(bf16[576,720]{1,0:T(8,128)(2,1)} %get-tuple-element.5) | copy-start | bytes 2488324

commit v2 on v1

v2 whole, which is shorter than its diff:
```python
import functools
import math

import jax
import jax.numpy as jnp
import numpy as np
from jax import lax
from jax.experimental import pallas as pl
from jax.experimental.pallas import tpu as pltpu
from jax.sharding import PartitionSpec as P

ENS = 4
SMOOTH_SQ = 0.25
MESH = pl.DeviceIdType.MESH
F32 = jnp.float32
BF16 = jnp.bfloat16
LANES = 128
TILE = 16


def order_tables(lon_count, degree_total):
    phase = np.arange(degree_total)[:, None] * np.arange(lon_count)[None, :] % lon_count
    angle = phase.astype(np.float32) * np.float32(2.0 * math.pi / lon_count)
    paired = np.stack([np.cos(angle), -np.sin(angle)])
    forward = jnp.asarray((paired / np.float32(math.sqrt(lon_count))).astype(BF16))
    inverse = jnp.asarray((paired / np.float32(math.sqrt(degree_total))).astype(BF16))
    return forward, inverse


def nt_dot(a, b):
    return lax.dot_general(a, b, (((1,), (1,)), ((), ())), preferred_element_type=F32)


def kernel_slope(diff):
    return diff * lax.rsqrt(diff * diff + SMOOTH_SQ)


def kernel(
    sizes,
    field_hbm, orders_ref, order_row_ref, filter_ref, forward_hbm,
    inverse_hbm, target_hbm, analysis_hbm, synthesis_ref_hbm,
    pred_hbm, grad_hbm,
    field_ref, forward_ref, inverse_tab, target_ref, analysis_ref, synthesis_ref,
    analysis_t, filter_t, inverse_rows,
    send1, recv1, x0, x1, b0, b1, send2, recv2, pred_ref, members, slopes, grad_in,
    local_sem, out_sem, send1_sem, recv1_sem, send2_sem, recv2_sem,
    send3_sem, recv3_sem, send4_sem, recv4_sem,
):
    n, lat, chan, slots, groups, per_group, degrees, per_send, pair = sizes
    lat_total = n * lat
    padded = groups * TILE
    me = lax.axis_index("polar")
    slab = lax.axis_index("ens")
    member = lax.rem(slab, ENS)
    group_base = slab - member
    chunks = lat // pair
    rows = pair * chan
    quarter = rows // ENS

    pairs_in = [
        (forward_hbm, forward_ref),
        (field_hbm, field_ref),
        (analysis_hbm, analysis_ref),
        (inverse_hbm, inverse_tab),
        (synthesis_ref_hbm, synthesis_ref),
        (target_hbm, target_ref),
    ]
    local = [
        pltpu.make_async_copy(src, dst, local_sem.at[i]) for i, (src, dst) in enumerate(pairs_in)
    ]
    for copy in local:
        copy.start()

    barrier = pltpu.get_barrier_semaphore()

    @pl.loop(1, n)
    def _(step):
        pl.semaphore_signal(
            barrier, inc=1, device_id={"polar": lax.rem(me + step, n)}, device_id_type=MESH
        )

    for step in range(1, ENS):
        other = group_base + lax.rem(member + step, ENS)
        pl.semaphore_signal(barrier, inc=1, device_id={"ens": other}, device_id_type=MESH)

    def first_copy(slot, dest, group):
        return pltpu.make_async_remote_copy(
            src_ref=send1.at[group, dest],
            dst_ref=recv1.at[group, slot],
            send_sem=send1_sem.at[group, dest],
            recv_sem=recv1_sem.at[group, slot],
            device_id={"polar": dest},
            device_id_type=MESH,
        )

    def second_copy(slot, dest, chunk):
        return pltpu.make_async_remote_copy(
            src_ref=send2.at[chunk, dest],
            dst_ref=recv2.at[chunk, slot],
            send_sem=send2_sem.at[chunk, dest],
            recv_sem=recv2_sem.at[chunk, slot],
            device_id={"polar": dest},
            device_id_type=MESH,
        )

    def row_start(chunk, owner):
        return pl.multiple_of(chunk * rows + owner * quarter, TILE)

    def member_copy(slot, dest, chunk):
        return pltpu.make_async_remote_copy(
            src_ref=pred_ref.at[pl.ds(row_start(chunk, dest), quarter)],
            dst_ref=members.at[chunk, slot],
            send_sem=send3_sem.at[chunk, dest],
            recv_sem=recv3_sem.at[chunk, slot],
            device_id={"ens": group_base + dest},
            device_id_type=MESH,
        )

    def slope_copy(slot, dest, chunk):
        return pltpu.make_async_remote_copy(
            src_ref=slopes.at[chunk, dest],
            dst_ref=grad_in.at[pl.ds(row_start(chunk, slot), quarter)],
            send_sem=send4_sem.at[chunk, dest],
            recv_sem=recv4_sem.at[chunk, slot],
            device_id={"ens": group_base + dest},
            device_id_type=MESH,
        )

    def out_copy(which, chunk):
        source, dest = ((pred_ref, pred_hbm), (grad_in, grad_hbm))[which]
        at = pl.ds(chunk * rows, rows)
        return pltpu.make_async_copy(source.at[at], dest.at[at], out_sem.at[which, chunk])

    order_row = order_row_ref[...].astype(F32)

    def one_hot(device, group, rank):
        slot = group * per_group + rank
        live = (rank < per_group) & (slot < slots)
        slot = jnp.where(live, device * slots + slot, -1)
        ids = lax.broadcasted_iota(jnp.int32, (slot.shape[0], order_row.shape[1]), 1)
        picked = jnp.where(ids == slot, order_row + 1.0, 0.0)
        order = jnp.sum(picked, axis=1, keepdims=True) - 1.0
        ids = lax.broadcasted_iota(jnp.int32, (slot.shape[0], degrees), 1).astype(F32)
        return jnp.where(ids == order, 1.0, 0.0).astype(BF16)

    def selected(hot, table):
        return jnp.dot(hot, table, preferred_element_type=F32).astype(BF16)

    batches = n // per_send
    span = per_send * TILE

    def column(count):
        return lax.broadcasted_iota(jnp.int32, (count, 1), 0)

    def spectral(group, batch):
        first = batch * per_send
        position = column(span)
        hot = one_hot(first + position // TILE, group, lax.rem(position, TILE))
        table = jnp.concatenate([selected(hot, forward_ref[0]), selected(hot, forward_ref[1])], 0)
        values = nt_dot(table, field_ref[...])
        both = jnp.concatenate([values[:span], values[span:]], axis=1).astype(BF16)
        for j in range(per_send):
            send1[group, first + j] = both[j * TILE : (j + 1) * TILE]

    def dispatch(group, batch):
        first = batch * per_send

        @pl.loop(0, per_send)
        def _(j):
            dest = first + lax.rem(me + 1 + j, per_send)

            @pl.when(dest != me)
            def _():
                first_copy(me, dest, group).start()

    local[0].wait()
    local[1].wait()
    spectral(0, 0)
    pl.semaphore_wait(barrier, n - 1 + ENS - 1)
    dispatch(0, 0)

    @pl.loop(1, groups * batches)
    def _(i):
        spectral(i // batches, lax.rem(i, batches))
        dispatch(i // batches, lax.rem(i, batches))

    local[2].wait()

    @pl.loop(0, slots)
    def _(s):
        order = orders_ref[me * slots + s]
        table = jnp.transpose(analysis_ref[s].astype(F32))
        degree = lax.broadcasted_iota(jnp.int32, table.shape, 0)
        analysis_t[s] = jnp.where(degree >= order, table, 0.0).astype(BF16)

    turned = jnp.transpose(filter_ref[...])
    filter_t[...] = jnp.zeros_like(filter_t)
    filter_t[:, 0:chan] = turned
    filter_t[:, LANES : LANES + chan] = turned
    b0[...] = jnp.zeros_like(b0)
    b1[...] = jnp.zeros_like(b1)
    local[3].wait()
    local[4].wait()
    local[5].wait()

    def turn_inverse():
        @pl.loop(0, n)
        def _(device):
            position = column(padded)
            hot = one_hot(device, position // TILE, lax.rem(position, TILE))
            at = pl.ds(pl.multiple_of(device * padded, TILE), padded)
            inverse_rows[0, at] = selected(hot, inverse_tab[0])
            inverse_rows[1, at] = selected(hot, inverse_tab[1])

    turn_inverse()

    for group in range(groups):
        recv1[group, me] = send1[group, me]

        @pl.loop(0, n)
        def _(src):
            @pl.when(src != me)
            def _():
                first_copy(src, src, group).wait_recv()

            block = recv1[group, src].astype(F32)
            for t in range(lat):
                at = pl.ds(pl.multiple_of((src * lat + t) * TILE, TILE), TILE)
                x0[at, 0:chan] = block[:, t * chan : (t + 1) * chan]
                x1[at, 0:chan] = block[:, (lat + t) * chan : (lat + t + 1) * chan]

        base = group * lat_total * TILE

        def legendre(rank, carry):
            s = group * per_group + rank
            at = pl.ds(rank, lat_total, stride=TILE)
            values = jnp.concatenate([x0[at, :], x1[at, :]], axis=1).astype(BF16)
            coeffs = jnp.dot(analysis_t[s], values, preferred_element_type=F32)
            scaled = (coeffs * filter_t[...]).astype(BF16)
            bands = jnp.dot(synthesis_ref[s], scaled, preferred_element_type=F32)
            out = pl.ds(base + rank, lat_total, stride=TILE)
            b0[out, :] = bands[:, :LANES]
            b1[out, :] = bands[:, LANES:]
            return carry

        count = min(per_group, slots - group * per_group)
        unroll = max(u for u in (1, 2, 3, 4, 5) if count % u == 0)
        lax.fori_loop(0, count, legendre, 0, unroll=unroll)

        for chunk in range(chunks):

            @pl.loop(0, n)
            def _(step):
                dest = lax.rem(me + 1 + step, n)
                parts = []
                for source in (b0, b1):
                    for t in range(pair):
                        at = base + (dest * lat + chunk * pair + t) * TILE
                        parts.append(source[pl.ds(pl.multiple_of(at, TILE), TILE), 0:chan])
                send2[chunk, dest, group * TILE : (group + 1) * TILE, :] = jnp.concatenate(
                    parts, axis=1
                ).astype(BF16)

                if group == groups - 1:

                    @pl.when(dest != me)
                    def _():
                        second_copy(me, dest, chunk).start()

    def invert(chunk):
        recv2[chunk, me] = send2[chunk, me]

        @pl.loop(1, n)
        def _(step):
            src = lax.rem(me + step, n)
            second_copy(src, src, chunk).wait_recv()

        bands = recv2[chunk].reshape(n * padded, 2 * rows)
        turned = jnp.transpose(bands.astype(F32)).astype(BF16)
        synth = jnp.dot(turned[:rows], inverse_rows[0], preferred_element_type=F32)
        synth = synth + jnp.dot(turned[rows:], inverse_rows[1], preferred_element_type=F32)
        at = pl.ds(chunk * rows, rows)
        pred_ref[at, :] = (field_ref[at, :].astype(F32) + synth).astype(BF16)
        for step in range(1, ENS):
            member_copy(member, lax.rem(member + step, ENS), chunk).start()
        out_copy(0, chunk).start()

    def score(chunk):
        own = pl.ds(row_start(chunk, member), quarter)
        members[chunk, member] = pred_ref[own, :]
        for step in range(1, ENS):
            source = lax.rem(member + step, ENS)
            member_copy(source, source, chunk).wait_recv()

        @pl.loop(0, quarter // TILE)
        def _(i):
            start = pl.multiple_of(i * TILE, TILE)
            at = pl.ds(start, TILE)
            seen = target_ref[pl.ds(row_start(chunk, member) + start, TILE), :].astype(F32)
            values = [members[chunk, e, at, :].astype(F32) for e in range(ENS)]
            pairs = [jnp.zeros_like(seen) for _ in range(ENS)]
            for a in range(ENS):
                for b in range(a + 1, ENS):
                    slope = kernel_slope(values[a] - values[b])
                    pairs[a] = pairs[a] + slope
                    pairs[b] = pairs[b] - slope
            for e in range(ENS):
                total = kernel_slope(values[e] - seen) - pairs[e] / ENS
                slopes[chunk, e, at, :] = total.astype(BF16)

        for step in range(1, ENS):
            slope_copy(member, lax.rem(member + step, ENS), chunk).start()
        grad_in[own, :] = slopes[chunk, member]

    def collect(chunk):
        for step in range(1, ENS):
            other = lax.rem(member + step, ENS)
            slope_copy(other, other, chunk).wait_recv()
        out_copy(1, chunk).start()

    for chunk in range(chunks):
        invert(chunk)
        if chunk:
            score(chunk - 1)
    score(chunks - 1)

    @pl.loop(1, n)
    def _(step):
        dest = lax.rem(me + step, n)
        for group in range(groups):
            first_copy(me, dest, group).wait_send()
        for chunk in range(chunks):
            second_copy(me, dest, chunk).wait_send()

    for chunk in range(chunks):
        collect(chunk)
    for chunk in range(chunks):
        for step in range(1, ENS):
            other = lax.rem(member + step, ENS)
            member_copy(member, other, chunk).wait_send()
            slope_copy(member, other, chunk).wait_send()
        out_copy(0, chunk).wait()
        out_copy(1, chunk).wait()


def body(field, target, slot_orders, analysis, synthesis, degree_filter):
    lat, chan, lon = field.shape[1:]
    slots, lat_total, degrees = analysis.shape
    n = lax.axis_size("polar")
    group_count = lax.axis_size("ens") // ENS
    groups = -(-slots // TILE)
    per_group = -(-slots // groups)
    padded = groups * TILE
    per_send = max(d for d in range(1, n + 1) if n % d == 0 and (d == 1 or d * TILE <= 128))
    pair = 2 if lat % 2 == 0 else 1
    chunks = lat // pair
    rows = pair * chan
    quarter = rows // ENS
    forward, inverse = order_tables(lon, degrees)
    observed = target
    filters = degree_filter
    if group_count > 1:
        start = lax.axis_index("ens") // ENS * chan
        observed = lax.dynamic_slice_in_dim(target, start, chan, 1)
        filters = lax.dynamic_slice_in_dim(degree_filter, start, chan, 0)
    sizes = (n, lat, chan, slots, groups, per_group, degrees, per_send, pair)
    vmem = pl.BlockSpec(memory_space=pltpu.VMEM)
    smem = pl.BlockSpec(memory_space=pltpu.SMEM)
    anywhere = pl.BlockSpec(memory_space=pl.ANY)
    dma = pltpu.SemaphoreType.DMA
    flat = jax.ShapeDtypeStruct((lat * chan, lon), BF16)
    prediction, gradient = pl.pallas_call(
        functools.partial(kernel, sizes),
        out_shape=(flat, flat),
        in_specs=[anywhere, smem, vmem, vmem] + [anywhere] * 5,
        out_specs=(anywhere, anywhere),
        scratch_shapes=[
            pltpu.VMEM((lat * chan, lon), BF16),
            pltpu.VMEM(forward.shape, BF16),
            pltpu.VMEM(inverse.shape, BF16),
            pltpu.VMEM((lat * chan, lon), BF16),
            pltpu.VMEM(analysis.shape, BF16),
            pltpu.VMEM((slots, lat_total, degrees), BF16),
            pltpu.VMEM((slots, degrees, lat_total), BF16),
            pltpu.VMEM((degrees, 2 * LANES), F32),
            pltpu.VMEM((2, n * padded, lon), BF16),
            pltpu.VMEM((groups, n, TILE, 2 * lat * chan), BF16),
            pltpu.VMEM((groups, n, TILE, 2 * lat * chan), BF16),
            pltpu.VMEM((lat_total * TILE, LANES), F32),
            pltpu.VMEM((lat_total * TILE, LANES), F32),
            pltpu.VMEM((groups * lat_total * TILE, LANES), F32),
            pltpu.VMEM((groups * lat_total * TILE, LANES), F32),
            pltpu.VMEM((chunks, n, padded, 2 * rows), BF16),
            pltpu.VMEM((chunks, n, padded, 2 * rows), BF16),
            pltpu.VMEM((lat * chan, lon), BF16),
            pltpu.VMEM((chunks, ENS, quarter, lon), BF16),
            pltpu.VMEM((chunks, ENS, quarter, lon), BF16),
            pltpu.VMEM((lat * chan, lon), BF16),
            dma((6,)),
            dma((2, chunks)),
            dma((groups, n)),
            dma((groups, n)),
            dma((chunks, n)),
            dma((chunks, n)),
            dma((chunks, ENS)),
            dma((chunks, ENS)),
            dma((chunks, ENS)),
            dma((chunks, ENS)),
        ],
        compiler_params=pltpu.CompilerParams(
            collective_id=0, has_side_effects=True, vmem_limit_bytes=56 * 1024 * 1024
        ),
    )(
        field.reshape(lat * chan, lon),
        slot_orders,
        slot_orders.reshape(1, -1),
        filters,
        forward,
        inverse,
        observed.reshape(lat * chan, lon),
        analysis,
        jnp.swapaxes(synthesis, 1, 2),
    )
    return prediction.reshape(field.shape), gradient.reshape(field.shape)


def solution(mesh):
    in_specs = (
        P("ens", "polar", None, None),
        P("polar", None, None),
        P(),
        P("polar", None, None),
        P("polar", None, None),
        P(),
    )
    out_specs = (P("ens", "polar", None, None), P("ens", "polar", None, None))
    return jax.shard_map(body, mesh=mesh, in_specs=in_specs, out_specs=out_specs, check_vma=False)
```

time: 88.5 us -> 75.4 us (0.85)
  the two profiles are of different devices: /device:TPU:13 before, /device:TPU:25 now
where the time goes in v2:
time: 75.4 us; the launch traced here: 75.2 us
  Pallas kernels  70.2 us (93%)
  local copies, waits for them, and re-layouts  4.38 us (6%)
    pallas_call x1, Pallas kernels, body(): pl.pallas_call(functools.partial(kernel, sizes), out_shape=(flat, flat),...  70.2 us
    unnamed x4, local copies, waits for them, and re-layouts  3.13 us

profile of v2, /device:TPU:25, one launch (start us, length us, event | category | flops | bytes accessed | tf_op | source)
XLA Modules:
  0.0 75.2 jit_solution(17754102583571409769)
XLA Ops:
  0.6 1.2 %reshape.20.order_row_ref = s32[1,360]{1,0:T(1,128)} reshape(s32[360]{0:T(512)} %orders_ref.1) | data formatting | bytes 2880 | tf_op jit(solution)/shard_map/reshape | solution.py:416
  1.9 70.2 %shard_map.95 = (bf16[576,720]{1,0:T(8,128)(2,1)}, bf16[576,720]{1,0:T(8,128)(2,1)}) custom-call(bf16[576,720]{1,0:T(8,128)(2,1)} %bitcast.8, s32[360]{0:T(512)} %orders_ref.1, s32[1,360]{1,0:T(1,128)} %reshape.20.order_row_ref, f32[96,360]{1,0:T(8,128)} %filter_ref.1, bf16[2,360,720]{2,1,0:T(8,128)(2,1)} %constant.4.clone.forward_hbm, ...), custom_call_target="tpu_custom_call" | custom-call | tf_op jit(solution)/shard_map/pallas_call | solution.py:372
  72.1 0.0 copy-start
  72.1 2.2 %copy.12 = bf16[1,6,96,720]{3,2,1,0:T(8,128)(2,1)} copy(bf16[1,6,96,720]{3,2,1,0:T(8,128)(2,1)} %bitcast.7) | data formatting | bytes 1658880
  74.3 0.0 copy-done
  74.3 0.9 %copy.13 = bf16[1,6,96,720]{3,2,1,0:T(8,128)(2,1)} copy(bf16[1,6,96,720]{3,2,1,0:T(8,128)(2,1)S(1)} %bitcast.6) | data formatting | bytes 1658880
Async XLA Ops:
  72.1 2.2 %copy-start = (bf16[576,720]{1,0:T(8,128)(2,1)S(1)}, bf16[576,720]{1,0:T(8,128)(2,1)}, u32[]{:S(2)}) copy-start(bf16[576,720]{1,0:T(8,128)(2,1)} %get-tuple-element.5) | copy-start | bytes 2488324

commit v3 on v2

--- a/solution.py
+++ b/solution.py
@@ -184,14 +184,13 @@
         spectral(i // batches, lax.rem(i, batches))
         dispatch(i // batches, lax.rem(i, batches))
 
-    local[2].wait()
-
-    @pl.loop(0, slots)
-    def _(s):
-        order = orders_ref[me * slots + s]
-        table = jnp.transpose(analysis_ref[s].astype(F32))
-        degree = lax.broadcasted_iota(jnp.int32, table.shape, 0)
-        analysis_t[s] = jnp.where(degree >= order, table, 0.0).astype(BF16)
+    def turn_analysis(group):
+        @pl.loop(group * per_group, min(slots, (group + 1) * per_group))
+        def _(s):
+            order = orders_ref[me * slots + s]
+            table = jnp.transpose(analysis_ref[s].astype(F32))
+            degree = lax.broadcasted_iota(jnp.int32, table.shape, 0)
+            analysis_t[s] = jnp.where(degree >= order, table, 0.0).astype(BF16)
 
     turned = jnp.transpose(filter_ref[...])
     filter_t[...] = jnp.zeros_like(filter_t)
@@ -199,22 +198,23 @@
     filter_t[:, LANES : LANES + chan] = turned
     b0[...] = jnp.zeros_like(b0)
     b1[...] = jnp.zeros_like(b1)
-    local[3].wait()
+    local[2].wait()
     local[4].wait()
-    local[5].wait()
 
     def turn_inverse():
-        @pl.loop(0, n)
-        def _(device):
-            position = column(padded)
-            hot = one_hot(device, position // TILE, lax.rem(position, TILE))
-            at = pl.ds(pl.multiple_of(device * padded, TILE), padded)
+        span = per_send * padded
+
+        @pl.loop(0, batches)
+        def _(batch):
+            position = column(span)
+            place = lax.rem(position, padded)
+            hot = one_hot(batch * per_send + position // padded, place // TILE, lax.rem(place, TILE))
+            at = pl.ds(pl.multiple_of(batch * span, TILE), span)
             inverse_rows[0, at] = selected(hot, inverse_tab[0])
             inverse_rows[1, at] = selected(hot, inverse_tab[1])
 
-    turn_inverse()
-
     for group in range(groups):
+        turn_analysis(group)
         recv1[group, me] = send1[group, me]
 
         @pl.loop(0, n)
@@ -266,6 +266,10 @@
                     @pl.when(dest != me)
                     def _():
                         second_copy(me, dest, chunk).start()
+
+    local[3].wait()
+    local[5].wait()
+    turn_inverse()
 
     def invert(chunk):
         recv2[chunk, me] = send2[chunk, me]
@@ -341,6 +345,19 @@
             slope_copy(member, other, chunk).wait_send()
         out_copy(0, chunk).wait()
         out_copy(1, chunk).wait()
+
+
+def copy_kernel(pieces, pred_hbm, grad_hbm, pred_out, grad_out, sem):
+    part = pred_hbm.shape[0] // pieces
+    copies = []
+    for which, (source, dest) in enumerate(((pred_hbm, pred_out), (grad_hbm, grad_out))):
+        for i in range(pieces):
+            at = pl.ds(i * part, part)
+            copies.append(pltpu.make_async_copy(source.at[at], dest.at[at], sem.at[which, i]))
+    for copy in copies:
+        copy.start()
+    for copy in copies:
+        copy.wait()
 
 
 def body(field, target, slot_orders, analysis, synthesis, degree_filter):
@@ -421,6 +438,14 @@
         analysis,
         jnp.swapaxes(synthesis, 1, 2),
     )
+    pieces = lat
+    prediction, gradient = pl.pallas_call(
+        functools.partial(copy_kernel, pieces),
+        out_shape=(flat, flat),
+        in_specs=[anywhere] * 2,
+        out_specs=(anywhere, anywhere),
+        scratch_shapes=[dma((2, pieces))],
+    )(prediction, gradient)
     return prediction.reshape(field.shape), gradient.reshape(field.shape)
 
 

time: 75.4 us -> 128 us (1.70)
  Pallas kernels: 70.2 us -> 126 us
  local copies, waits for them, and re-layouts: 4.38 us -> 1.25 us
    pallas_call x0 -> x1, Pallas kernels: none -> 54.8 us  [body(): pl.pallas_call(functools.partial(copy_kernel, pieces), out_shape=(flat, f...]
    unnamed x4 -> x0, local copies, waits for them, and re-layouts: 3.13 us -> none
where the time goes in v3:
time: 128 us; the launch traced here: 127 us
  Pallas kernels  126 us (98%)
    pallas_call x1, Pallas kernels, body(): pl.pallas_call(functools.partial(kernel, sizes), out_shape=(flat, flat),...  70.7 us
    pallas_call x1, Pallas kernels, body(): pl.pallas_call(functools.partial(copy_kernel, pieces), out_shape=(flat, f...  54.8 us

profile of v3, /device:TPU:25, one launch (start us, length us, event | category | flops | bytes accessed | tf_op | source)
XLA Modules:
  0.0 127.4 jit_solution(14159299455933487848)
XLA Ops:
  0.6 1.2 reshape.20.order_row_ref
  1.9 70.7 %shard_map.95 = (bf16[576,720]{1,0:T(8,128)(2,1)}, bf16[576,720]{1,0:T(8,128)(2,1)}) custom-call(bf16[576,720]{1,0:T(8,128)(2,1)} %bitcast.6, s32[360]{0:T(512)} %orders_ref.1, s32[1,360]{1,0:T(1,128)} %reshape.20.order_row_ref, f32[96,360]{1,0:T(8,128)} %filter_ref.1, bf16[2,360,720]{2,1,0:T(8,128)(2,1)} %constant.4.clone.forward_hbm, ...), custom_call_target="tpu_custom_call" | custom-call | tf_op jit(solution)/shard_map/pallas_call | solution.py:389
  72.6 54.8 %shard_map.96 = (bf16[576,720]{1,0:T(8,128)(2,1)}, bf16[576,720]{1,0:T(8,128)(2,1)}) custom-call(bf16[576,720]{1,0:T(8,128)(2,1)} %get-tuple-element.6.pred_hbm, bf16[576,720]{1,0:T(8,128)(2,1)} %get-tuple-element.7.grad_hbm), custom_call_target="tpu_custom_call" | custom-call | tf_op jit(solution)/shard_map/pallas_call | solution.py:442

commit v4 on v3

--- a/solution.py
+++ b/solution.py
@@ -93,15 +93,20 @@
             device_id_type=MESH,
         )
 
-    def second_copy(slot, dest, chunk):
+    def second_copy(slot, dest, chunk, part):
+        sem = part if chunk == 0 else groups + chunk - 1
+        at = pl.ds(part * TILE, TILE) if chunk == 0 else pl.ds(0, padded)
         return pltpu.make_async_remote_copy(
-            src_ref=send2.at[chunk, dest],
-            dst_ref=recv2.at[chunk, slot],
-            send_sem=send2_sem.at[chunk, dest],
-            recv_sem=recv2_sem.at[chunk, slot],
+            src_ref=send2.at[chunk, dest, at],
+            dst_ref=recv2.at[chunk, slot, at],
+            send_sem=send2_sem.at[sem, dest],
+            recv_sem=recv2_sem.at[sem, slot],
             device_id={"polar": dest},
             device_id_type=MESH,
         )
+
+    def parts_of(chunk):
+        return range(groups if chunk == 0 else 1)
 
     def row_start(chunk, owner):
         return pl.multiple_of(chunk * rows + owner * quarter, TILE)
@@ -261,15 +266,16 @@
                     parts, axis=1
                 ).astype(BF16)
 
-                if group == groups - 1:
+                if chunk == 0 or group == groups - 1:
 
                     @pl.when(dest != me)
                     def _():
-                        second_copy(me, dest, chunk).start()
-
-    local[3].wait()
-    local[5].wait()
-    turn_inverse()
+                        second_copy(me, dest, chunk, group).start()
+
+        if group == 0:
+            local[3].wait()
+            local[5].wait()
+            turn_inverse()
 
     def invert(chunk):
         recv2[chunk, me] = send2[chunk, me]
@@ -277,7 +283,8 @@
         @pl.loop(1, n)
         def _(step):
             src = lax.rem(me + step, n)
-            second_copy(src, src, chunk).wait_recv()
+            for part in parts_of(chunk):
+                second_copy(src, src, chunk, part).wait_recv()
 
         bands = recv2[chunk].reshape(n * padded, 2 * rows)
         turned = jnp.transpose(bands.astype(F32)).astype(BF16)
@@ -334,7 +341,8 @@
         for group in range(groups):
             first_copy(me, dest, group).wait_send()
         for chunk in range(chunks):
-            second_copy(me, dest, chunk).wait_send()
+            for part in parts_of(chunk):
+                second_copy(me, dest, chunk, part).wait_send()
 
     for chunk in range(chunks):
         collect(chunk)
@@ -345,19 +353,6 @@
             slope_copy(member, other, chunk).wait_send()
         out_copy(0, chunk).wait()
         out_copy(1, chunk).wait()
-
-
-def copy_kernel(pieces, pred_hbm, grad_hbm, pred_out, grad_out, sem):
-    part = pred_hbm.shape[0] // pieces
-    copies = []
-    for which, (source, dest) in enumerate(((pred_hbm, pred_out), (grad_hbm, grad_out))):
-        for i in range(pieces):
-            at = pl.ds(i * part, part)
-            copies.append(pltpu.make_async_copy(source.at[at], dest.at[at], sem.at[which, i]))
-    for copy in copies:
-        copy.start()
-    for copy in copies:
-        copy.wait()
 
 
 def body(field, target, slot_orders, analysis, synthesis, degree_filter):
@@ -417,8 +412,8 @@
             dma((2, chunks)),
             dma((groups, n)),
             dma((groups, n)),
-            dma((chunks, n)),
-            dma((chunks, n)),
+            dma((groups + chunks - 1, n)),
+            dma((groups + chunks - 1, n)),
             dma((chunks, ENS)),
             dma((chunks, ENS)),
             dma((chunks, ENS)),
@@ -438,14 +433,6 @@
         analysis,
         jnp.swapaxes(synthesis, 1, 2),
     )
-    pieces = lat
-    prediction, gradient = pl.pallas_call(
-        functools.partial(copy_kernel, pieces),
-        out_shape=(flat, flat),
-        in_specs=[anywhere] * 2,
-        out_specs=(anywhere, anywhere),
-        scratch_shapes=[dma((2, pieces))],
-    )(prediction, gradient)
     return prediction.reshape(field.shape), gradient.reshape(field.shape)
 
 

time: 128 us -> 73.1 us (0.57)
  Pallas kernels: 126 us -> 67.9 us
  local copies, waits for them, and re-layouts: 1.25 us -> 4.38 us
    pallas_call x1 -> x0, Pallas kernels: 54.8 us -> none  [body(): pl.pallas_call(functools.partial(copy_kernel, pieces), out_shape=(flat, f...]
    unnamed x0 -> x4, local copies, waits for them, and re-layouts: none -> 3.13 us
    pallas_call x1, Pallas kernels: 70.7 us -> 67.9 us  [body(): pl.pallas_call(functools.partial(kernel, sizes), out_shape=(flat, flat),...]
where the time goes in v4:
time: 73.1 us; the launch traced here: 72.9 us
  Pallas kernels  67.9 us (93%)
  local copies, waits for them, and re-layouts  4.38 us (6%)
    pallas_call x1, Pallas kernels, body(): pl.pallas_call(functools.partial(kernel, sizes), out_shape=(flat, flat),...  67.9 us
    unnamed x4, local copies, waits for them, and re-layouts  3.13 us

profile of v4, /device:TPU:25, one launch (start us, length us, event | category | flops | bytes accessed | tf_op | source)
XLA Modules:
  0.0 72.9 jit_solution(10908654312362662198)
XLA Ops:
  0.6 1.2 %reshape.20.order_row_ref = s32[1,360]{1,0:T(1,128)} reshape(s32[360]{0:T(512)} %orders_ref.1) | data formatting | bytes 2880 | tf_op jit(solution)/shard_map/reshape | solution.py:428
  1.9 67.9 %shard_map.95 = (bf16[576,720]{1,0:T(8,128)(2,1)}, bf16[576,720]{1,0:T(8,128)(2,1)}) custom-call(bf16[576,720]{1,0:T(8,128)(2,1)} %bitcast.8, s32[360]{0:T(512)} %orders_ref.1, s32[1,360]{1,0:T(1,128)} %reshape.20.order_row_ref, f32[96,360]{1,0:T(8,128)} %filter_ref.1, bf16[2,360,720]{2,1,0:T(8,128)(2,1)} %constant.4.clone.forward_hbm, ...), custom_call_target="tpu_custom_call" | custom-call | tf_op jit(solution)/shard_map/pallas_call | solution.py:384
  69.8 0.0 copy-start
  69.8 2.2 %copy.12 = bf16[1,6,96,720]{3,2,1,0:T(8,128)(2,1)} copy(bf16[1,6,96,720]{3,2,1,0:T(8,128)(2,1)} %bitcast.7) | data formatting | bytes 1658880
  72.0 0.0 copy-done
  72.0 0.9 %copy.13 = bf16[1,6,96,720]{3,2,1,0:T(8,128)(2,1)} copy(bf16[1,6,96,720]{3,2,1,0:T(8,128)(2,1)S(1)} %bitcast.6) | data formatting | bytes 1658880
Async XLA Ops:
  69.8 2.2 %copy-start = (bf16[576,720]{1,0:T(8,128)(2,1)S(1)}, bf16[576,720]{1,0:T(8,128)(2,1)}, u32[]{:S(2)}) copy-start(bf16[576,720]{1,0:T(8,128)(2,1)} %get-tuple-element.5) | copy-start | bytes 2488324

commit v5 on v4

--- a/solution.py
+++ b/solution.py
@@ -331,9 +331,7 @@
 
     for chunk in range(chunks):
         invert(chunk)
-        if chunk:
-            score(chunk - 1)
-    score(chunks - 1)
+        score(chunk)
 
     @pl.loop(1, n)
     def _(step):

time: 73.1 us -> 79 us (1.081)
  Pallas kernels: 67.9 us -> 73.6 us
    pallas_call x1, Pallas kernels: 67.9 us -> 73.6 us  [body(): pl.pallas_call(functools.partial(kernel, sizes), out_shape=(flat, flat),...]
where the time goes in v5:
time: 79 us; the launch traced here: 78.7 us
  Pallas kernels  73.6 us (93%)
  local copies, waits for them, and re-layouts  4.38 us (6%)
    pallas_call x1, Pallas kernels, body(): pl.pallas_call(functools.partial(kernel, sizes), out_shape=(flat, flat),...  73.6 us
    unnamed x4, local copies, waits for them, and re-layouts  3.13 us

profile of v5, /device:TPU:25, one launch (start us, length us, event | category | flops | bytes accessed | tf_op | source)
XLA Modules:
  0.0 78.7 jit_solution(6669092815163039775)
XLA Ops:
  0.6 1.2 %reshape.20.order_row_ref = s32[1,360]{1,0:T(1,128)} reshape(s32[360]{0:T(512)} %orders_ref.1) | data formatting | bytes 2880 | tf_op jit(solution)/shard_map/reshape | solution.py:426
  1.9 73.6 %shard_map.95 = (bf16[576,720]{1,0:T(8,128)(2,1)}, bf16[576,720]{1,0:T(8,128)(2,1)}) custom-call(bf16[576,720]{1,0:T(8,128)(2,1)} %bitcast.8, s32[360]{0:T(512)} %orders_ref.1, s32[1,360]{1,0:T(1,128)} %reshape.20.order_row_ref, f32[96,360]{1,0:T(8,128)} %filter_ref.1, bf16[2,360,720]{2,1,0:T(8,128)(2,1)} %constant.4.clone.forward_hbm, ...), custom_call_target="tpu_custom_call" | custom-call | tf_op jit(solution)/shard_map/pallas_call | solution.py:382
  75.5 0.0 copy-start
  75.5 2.2 %copy.12 = bf16[1,6,96,720]{3,2,1,0:T(8,128)(2,1)} copy(bf16[1,6,96,720]{3,2,1,0:T(8,128)(2,1)} %bitcast.7) | data formatting | bytes 1658880
  77.7 0.0 copy-done
  77.7 0.9 %copy.13 = bf16[1,6,96,720]{3,2,1,0:T(8,128)(2,1)} copy(bf16[1,6,96,720]{3,2,1,0:T(8,128)(2,1)S(1)} %bitcast.6) | data formatting | bytes 1658880
Async XLA Ops:
  75.5 2.2 %copy-start = (bf16[576,720]{1,0:T(8,128)(2,1)S(1)}, bf16[576,720]{1,0:T(8,128)(2,1)}, u32[]{:S(2)}) copy-start(bf16[576,720]{1,0:T(8,128)(2,1)} %get-tuple-element.5) | copy-start | bytes 2488324
